TPU v7x, 128 devices: a whole 4x4x4 slice. The times are simulated.
128 devices in a mesh: dp: 8 (over x, core), fsdp: 16 (over z, y).
Axes of the slice: x: 4, y: 4, z: 4, core: 2. Of those that a mesh axis runs over, the one named last changes fastest.
Arguments:
- context: bfloat16 [65536, 8192], P(('dp', 'fsdp')), may hold values from -24 to 24
- cotangent: bfloat16 [65536, 1024], P(('dp', 'fsdp')), may hold values from -6 to 6
- out_weight: bfloat16 [8192, 1024], P('fsdp'), may hold values from -0.0625 to 0.0625
- error_memory: bfloat16 [8, 8192, 1024], P('dp', 'fsdp'), may hold values from -30 to 30, as said below
- seed_factor: float32 [4, 1024], replicated, may hold values from -0.1875 to 0.1875
Outputs:
- context_grad: bfloat16 [65536, 8192], P(('dp', 'fsdp'))
- new_memory: bfloat16 [8, 8192, 1024], P('dp', 'fsdp')
- right_factor: float32 [4, 1024], replicated
Inputs may be any that keep to these rules, and one draw needn't show every extreme that they name: `error_memory`: entries of the error memories.
All inputs are finite; a program needn't handle non-finite values.
Results may differ from a plain program's by a relative error of at most 0.011.
Values may be sent and summed in bfloat16 or wider, within the bound.
A program may use at most 128 MiB of HBM per device.

v0:
```python
import jax
import jax.numpy as jnp
from jax import lax
from jax.sharding import PartitionSpec as P

EPSILON = 1e-06
HIGH = lax.Precision.HIGHEST


def shards(context, cotangent, out_weight, error_memory, seed_factor):
    tok_count = context.shape[0]
    groups = lax.axis_size("fsdp")
    context_grad = lax.dot_general(
        cotangent,
        lax.all_gather(out_weight, "fsdp", axis=0, tiled=True),
        (((1,), (1,)), ((), ())),
        preferred_element_type=jnp.float32,
    ).astype(jnp.bfloat16)
    gradient = lax.psum_scatter(
        lax.dot_general(
            context, cotangent, (((0,), (0,)), ((), ())), preferred_element_type=jnp.float32
        ).astype(jnp.bfloat16),
        "fsdp",
        scatter_dimension=0,
        tiled=True,
    ).astype(jnp.float32)
    scale = 1.0 / jnp.sqrt(jnp.float32(tok_count * groups))
    memory = gradient * scale + error_memory[0].astype(jnp.float32)
    left_local = lax.dot_general(seed_factor, memory, (((1,), (1,)), ((), ())), precision=HIGH)
    p_sum = lax.psum(left_local, "dp")
    basis = []
    for column in range(p_sum.shape[0]):
        vector = p_sum[column]
        if column > 0:
            stacked = jnp.stack(basis)
            coeffs = lax.psum(jnp.dot(stacked, vector, precision=HIGH), "fsdp")
            vector = vector - jnp.dot(coeffs, stacked, precision=HIGH)
        squared = lax.psum(jnp.sum(vector * vector), "fsdp")
        basis.append(vector / jnp.sqrt(squared + EPSILON))
    p_hat = jnp.stack(basis)
    right_local = jnp.dot(p_hat, memory, precision=HIGH)
    right_factor = lax.psum(right_local, ("dp", "fsdp")) / lax.axis_size("dp")
    approx = lax.dot_general(p_hat, right_factor, (((0,), (0,)), ((), ())), precision=HIGH)
    new_memory = (memory - approx).astype(jnp.bfloat16)[None]
    return (context_grad, new_memory, right_factor)


def solution(mesh):
    placed = (
        P(("dp", "fsdp"), None),
        P(("dp", "fsdp"), None),
        P("fsdp", None),
        P("dp", "fsdp", None),
        P(),
    )
    return jax.shard_map(
        shards,
        mesh=mesh,
        in_specs=placed,
        out_specs=(P(("dp", "fsdp"), None), P("dp", "fsdp", None), P()),
        check_vma=False,
    )
```

profile of v0, /device:TPU:1, one launch (start us, length us, event | category | flops | bytes accessed | tf_op | source)
XLA Modules:
  0.0 529.0 jit_solution(1998652724904285845)
XLA Ops:
  7.2 1.2 copy-done
  8.4 15.9 %convolution_convert_fusion = bf16[8192,1024]{1,0:T(8,128)(2,1)} fusion(bf16[512,8192]{1,0:T(8,128)(2,1)} %param.5, bf16[512,1024]{1,0:T(8,128)(2,1)S(1)} %copy-done), kind=kOutput, calls=%fused_computation | convolution fusion | flops 8598323200 | bytes 26214400 | tf_op jit(solution)/shard_map/dot_general | solution.py:20
  24.4 0.7 all-gather.2.cloned.1.call-update
  25.1 113.0 %reduce-scatter.2.cloned.1.call-done = bf16[512,1024]{1,0:T(8,128)(2,1)} async-done(((bf16[8192,1024]{1,0:T(8,128)(2,1)}), bf16[512,1024]{1,0:T(8,128)(2,1)}) %reduce-scatter.2.cloned.1.call-update) | async-done | bytes 1048592 | tf_op jit(solution)/shard_map/reduce_scatter | solution.py:19
  138.1 3.3 fusion.3
  141.4 13.0 %psum.63 = f32[4,512]{1,0:T(4,128)S(1)} all-reduce(f32[4,512]{1,0:T(4,128)S(1)} %fusion.3), channel_id=1, replica_groups=mesh['dp'=8,'fsdp'=16] {'dp'}, use_global_device_ids=true, to_apply=%region_1.0 | all-reduce | flops 2048 | bytes 16384 | tf_op jit(solution)/shard_map/psum | solution.py:30
  154.4 0.6 multiply_reduce_fusion.4
  155.1 32.4 %psum.64 = f32[]{:T(128)} all-reduce(f32[]{:T(128)} %multiply_reduce_fusion.4), channel_id=1, replica_groups=mesh['dp'=8,'fsdp'=16] {'fsdp'}, use_global_device_ids=true, to_apply=%region_3.0 | all-reduce | flops 1 | bytes 8 | tf_op jit(solution)/shard_map/psum | solution.py:38
  188.2 0.6 multiply_reduce_fusion
  188.8 29.6 %psum.65 = f32[]{:T(128)} all-reduce(f32[]{:T(128)} %multiply_reduce_fusion), channel_id=1, replica_groups=mesh['dp'=8,'fsdp'=16] {'fsdp'}, use_global_device_ids=true, to_apply=%region_4.0 | all-reduce | flops 1 | bytes 8 | tf_op jit(solution)/shard_map/psum | solution.py:36
  218.4 1.2 multiply_reduce_fusion.3
  219.7 32.4 %psum.66 = f32[]{:T(128)} all-reduce(f32[]{:T(128)} %multiply_reduce_fusion.3), channel_id=1, replica_groups=mesh['dp'=8,'fsdp'=16] {'fsdp'}, use_global_device_ids=true, to_apply=%region_6.0 | all-reduce | flops 1 | bytes 8 | tf_op jit(solution)/shard_map/psum | solution.py:38
  252.8 0.7 broadcast_divide_fusion.2
  253.6 28.5 %psum.67 = f32[2]{0:T(128)S(1)} all-reduce(f32[2]{0:T(128)S(1)} %convolution_bitcast_fusion.1), channel_id=1, replica_groups=mesh['dp'=8,'fsdp'=16] {'fsdp'}, use_global_device_ids=true, to_apply=%region_7.0 | all-reduce | flops 2 | bytes 16 | tf_op jit(solution)/shard_map/psum | solution.py:36
  282.3 0.6 multiply_reduce_fusion.2
  282.9 30.8 %psum.68 = f32[]{:T(128)} all-reduce(f32[]{:T(128)} %get-tuple-element.5), channel_id=1, replica_groups=mesh['dp'=8,'fsdp'=16] {'fsdp'}, use_global_device_ids=true, to_apply=%region_9.0 | all-reduce | flops 1 | bytes 8 | tf_op jit(solution)/shard_map/psum | solution.py:38
  314.4 0.1 convolution_bitcast_fusion
  314.6 29.7 %convolution_convert_fusion.1 = bf16[512,8192]{1,0:T(8,128)(2,1)} fusion(bf16[512,1024]{1,0:T(8,128)(2,1)S(1)} %copy-done, bf16[8192,1024]{1,0:T(8,128)(2,1)} %all-gather.2.cloned.1.call-done), kind=kOutput, calls=%fused_computation.1 | convolution fusion | flops 8594128896 | bytes 26214400 | tf_op jit(solution)/shard_map/dot_general | solution.py:13
  344.3 28.5 %psum.69 = f32[3]{0:T(128)S(1)} all-reduce(f32[3]{0:T(128)S(1)} %convolution_bitcast_fusion), channel_id=1, replica_groups=mesh['dp'=8,'fsdp'=16] {'fsdp'}, use_global_device_ids=true, to_apply=%region_10.0 | all-reduce | flops 3 | bytes 24 | tf_op jit(solution)/shard_map/psum | solution.py:36
  372.9 0.6 multiply_reduce_fusion.1
  373.5 30.7 %psum.70 = f32[]{:T(128)} all-reduce(f32[]{:T(128)} %get-tuple-element.3), channel_id=1, replica_groups=mesh['dp'=8,'fsdp'=16] {'fsdp'}, use_global_device_ids=true, to_apply=%region_12.0 | all-reduce | flops 1 | bytes 8 | tf_op jit(solution)/shard_map/psum | solution.py:38
  405.0 1.3 fusion
  406.3 112.8 %psum.71 = f32[4,1024]{1,0:T(4,128)S(1)} all-reduce(f32[4,1024]{1,0:T(4,128)S(1)} %fusion), channel_id=1, replica_groups=mesh['dp'=8,'fsdp'=16] {'dp','fsdp'}, use_global_device_ids=true, to_apply=%region_13.0 | all-reduce | flops 4096 | bytes 32768 | tf_op jit(solution)/shard_map/psum | solution.py:42
  519.1 3.0 fusion.2
  (20 shorter events, 0.6 us)
Async XLA Ops:
  7.2 1.2 copy-start
  7.2 130.9 %reduce-scatter.2.cloned.1.call-start = ((), (), s32[]{:S(2)}) async-start(), calls=%async_computation.2 | async-start | bytes 17825792 | tf_op jit(solution)/shard_map/reduce_scatter | solution.py:19
  24.3 113.8 %copy-start.1 = (bf16[1,512,1024]{2,1,0:T(8,128)(2,1)S(1)}, bf16[1,512,1024]{2,1,0:T(8,128)(2,1)}, u32[]{:S(2)}) copy-start(bf16[1,512,1024]{2,1,0:T(8,128)(2,1)} %param.8) | copy-start | bytes 3145732
  24.3 113.8 %copy-start.4 = (f32[4,1024]{1,0:T(4,128)S(1)}, f32[4,1024]{1,0:T(4,128)}, u32[]{:S(2)}) copy-start(f32[4,1024]{1,0:T(4,128)} %param.9) | copy-start | bytes 49156
  24.3 290.2 %all-gather.2.cloned.1.call-start = ((), (), s32[]{:S(2)}) async-start(), calls=%async_computation.1 | async-start | bytes 17825792 | tf_op jit(solution)/shard_map/all_gather | solution.py:15
  314.6 90.4 %copy-start.2 = (bf16[512,1024]{1,0:T(8,128)(2,1)S(1)}, bf16[512,1024]{1,0:T(8,128)(2,1)}, u32[]{:S(2)}) copy-start(bf16[512,1024]{1,0:T(8,128)(2,1)} %reduce-scatter.2.cloned.1.call-done) | copy-start | bytes 3145732
  519.1 3.0 copy-start.3
Sparse Core Ops, SparseCore 0:
  24.5 113.6 reduce-scatter.1
  140.2 112.5 all-gather.1
where the time goes:
time: 529 us
  blocking collectives  339 us (64%)
  waiting for transfers between devices  114 us (22%)
  matrix products  53.9 us (10%)
  between operations  16.9 us (3%)
    psum x4, blocking collectives, shards(): squared = lax.psum(jnp.sum(vector * vector), 'fsdp')  126 us
    reduce_scatter x1, waiting for transfers between devices, shards(): lax.psum_scatter(lax.dot_general(context, cotangent, (((0,), (0,)), ((),...  113 us
    psum x1, blocking collectives, shards(): right_factor = lax.psum(right_local, ('dp', 'fsdp')) / lax.axis_size('dp')  113 us
    psum x3, blocking collectives, shards(): coeffs = lax.psum(jnp.dot(stacked, vector, precision=HIGH), 'fsdp')  86.6 us
    dot_general x1, matrix products, shards(): lax.dot_general(cotangent, lax.all_gather(out_weight, 'fsdp', axis=0, til...  29.7 us
    dot_general x1, matrix products, shards(): lax.dot_general(context, cotangent, (((0,), (0,)), ((), ())), preferred_e...  15.9 us
    psum x1, blocking collectives, shards(): p_sum = lax.psum(left_local, 'dp')  13 us
  transfers between devices with their start and end apart: 2, of which 1 were waited for; matrix products, arithmetic and copies ran while one was open for 1% of the time, Pallas kernels for 0%

commit v1 on v0

v1 whole, which is shorter than its diff:
```python
import functools

import jax
import jax.numpy as jnp
import numpy as np
from jax import lax
from jax.experimental import pallas as pl
from jax.experimental.pallas import tpu as pltpu
from jax.sharding import PartitionSpec as P

MESH = pl.DeviceIdType.MESH
F32 = jnp.float32
BF16 = jnp.bfloat16
EPSILON = 1e-06
TOK = 512
CH = 512
D = 1024
N_DP = 8
N_FSDP = 16
PIECE = 128
HALF = 512
SCALE = float(np.float32(1.0) / np.sqrt(np.float32(TOK * N_FSDP)))
EXCHANGE_ORDER = (0, 1, 4, 2, 5, 3, 6, 7)


def dot_tn(a, b):
    return lax.dot_general(a, b, (((0,), (0,)), ((), ())), preferred_element_type=F32)


def dot_nn(a, b):
    return lax.dot_general(a, b, (((1,), (0,)), ((), ())), preferred_element_type=F32)


def dot_nt(a, b):
    return lax.dot_general(a, b, (((1,), (1,)), ((), ())), preferred_element_type=F32)


def parts(v):
    hi = v.astype(BF16).astype(F32)
    rest = v - hi
    mid = rest.astype(BF16).astype(F32)
    return hi, mid, rest - mid


def stack(v):
    hi, mid, lo = parts(v)
    return jnp.concatenate([hi, mid, lo, jnp.zeros_like(hi)], axis=0).astype(BF16)


def fold(r):
    return r[0:8] + (r[8:16] + r[16:24])


def xor2(a, m):
    return ((a // 2 + m // 2) % 2) * 2 + (a % 2 + m % 2) % 2


def mask_of(i):
    return ((i + 1) % 3 + 1) * ((i + 2) // 3)


def kernel(
    seed_ref, cot_h, ctx_h, w_h, err_h,
    grad_h, newmem_ref, right_ref,
    ctx_v, cot_v, err_v, cotp, ctxp, s1s, s1r, rsend, opp, fin, wg, stage, base,
    ppart, rb1, rb2, rb3, pall, phat, rb5, rb6, rb7,
    lsem, osem, ssem, rsem,
):
    dp, fs = lax.axis_index("dp"), lax.axis_index("fsdp")
    x, c = dp // 2, dp % 2
    z, y = fs // 4, fs % 4
    a, b = z * (1 - c) + y * c, y * (1 - c) + z * c

    def fid(i, j):
        return (i * (1 - c) + j * c) * 4 + j * (1 - c) + i * c

    def at(i, j):
        return (dp, fid(i, j))

    aA, aB, bA, bB = xor2(a, 1), 3 - a, xor2(b, 1), 3 - b
    bP, bM = (b + 1) % 4, (b + 3) % 4
    xR, xL, xO = (x + 1) % 4, (x + 3) % 4, (x + 2) % 4
    right_chip, left_chip = (xR * 2 + c, fs), (xL * 2 + c, fs)
    sibling = (x * 2 + 1 - c, fs)
    border = [(b + k) % 4 for k in (2, 1, 3, 0)]
    row8 = lax.broadcasted_iota(jnp.int32, (8, CH), 0)

    cot_load = pltpu.make_async_copy(cot_h, cot_v, lsem.at[0])
    cot_load.start()
    for f in range(N_FSDP):
        pltpu.make_async_copy(ctx_h.at[:, pl.ds(f * CH, CH)], ctx_v.at[f], lsem.at[1]).start()
    err_load = pltpu.make_async_copy(err_h, err_v, lsem.at[2])
    err_load.start()
    my_rows, my_cols = pl.ds(pl.multiple_of(x * PIECE, PIECE), PIECE), pl.ds(pl.multiple_of(c * HALF, HALF), HALF)
    w_load = pltpu.make_async_copy(w_h.at[my_rows, my_cols], wg.at[a * 4 + b, my_rows, my_cols], lsem.at[3])
    w_load.start()

    barrier = pltpu.get_barrier_semaphore()
    peers = [((dp + i) % N_DP, fs) for i in range(1, N_DP)]
    peers += [(dp, ((z + i) % 4) * 4 + y) for i in range(1, 4)]
    peers += [(dp, z * 4 + (y + i) % 4) for i in range(1, 4)]
    for peer in peers:
        pl.semaphore_signal(barrier, inc=1, device_id=peer, device_id_type=MESH)
    pl.semaphore_wait(barrier, len(peers))

    sent = []

    def send(src, dst, device):
        n = len(sent)
        copy = pltpu.make_async_remote_copy(src, dst, ssem.at[n], rsem.at[n], device_id=device, device_id_type=MESH)
        copy.start()
        sent.append(copy)
        return copy

    def wslice(first, count, slot, core):
        return wg.at[
            pl.ds(first, count),
            pl.ds(pl.multiple_of(slot * PIECE, PIECE), PIECE),
            pl.ds(pl.multiple_of(core * HALF, HALF), HALF),
        ]

    def dp_exchange(src_of, buf):
        return [send(src_of((dp + i) % N_DP), buf.at[dp], ((dp + i) % N_DP, fs)) for i in range(1, N_DP)]

    def z_exchange(buf):
        return [send(buf.at[z], buf.at[z], (dp, ((z + i) % 4) * 4 + y)) for i in range(1, 4)]

    def y_exchange(buf):
        return [send(buf.at[y], buf.at[y], (dp, z * 4 + (y + i) % 4)) for i in range(1, 4)]

    def arrive(copies):
        for copy in copies:
            copy.wait_recv()

    def total(buf, n):
        t = buf[0]
        for i in range(1, n):
            t = t + buf[i]
        return t

    def product(f, j):
        return dot_tn(ctx_v[f], cot_v[...]) + dot_tn(ctxp[j], cotp[...])

    exchange = {}

    def send_columns(step):
        j = EXCHANGE_ORDER[step]
        owner = 3 - aA if j < 4 else aA
        exchange[j] = send(ctx_v.at[fid(owner, border[j % 4])], ctxp.at[j], at(aA, b))

    first = {}

    def make_first(k):
        exchange[k].wait_recv()
        s1s[k] = product(fid(aB, border[k]), k).astype(BF16)

    def send_first(k, half):
        rows = pl.ds(half * 256, 256)
        first[k, half] = send(s1s.at[k, rows], s1r.at[k, rows], at(aB, b))

    second = {}

    def make_second(k):
        exchange[4 + k].wait_recv()
        first[k, 0].wait_recv()
        first[k, 1].wait_recv()
        rsend[k] = (product(fid(a, border[k]), 4 + k) + s1r[k].astype(F32)).astype(BF16)

    low, high = pl.ds(0, 256), pl.ds(256, 256)

    ring = {}

    def group(i):
        return xor2(a, int(mask_of(i)))

    def x_own(i, part):
        src = wslice(group(i) * 4 + part * 2, 2, x, c)
        ring[i, part, "right"] = send(src, src, right_chip)
        ring[i, part, "left"] = send(src, src, left_chip)

    def x_forward(i):
        ring[i, 0, "right"].wait_recv()
        ring[i, 1, "left"].wait_recv()
        src = wslice(group(i) * 4, 2, xL, c)
        ring[i, 2, "right"] = send(src, src, right_chip)
        src = wslice(group(i) * 4 + 2, 2, xR, c)
        ring[i, 2, "left"] = send(src, src, left_chip)

    across = {}

    def x_finish(i):
        ring[i, 0, "left"].wait_recv()
        ring[i, 1, "right"].wait_recv()
        ring[i, 2, "right"].wait_recv()
        ring[i, 2, "left"].wait_recv()
        across[i] = [
            send(wg.at[group(i) * 4 + j, :, my_cols], wg.at[j * 4 + group(i), :, my_cols], sibling) for j in range(4)
        ]

    def out_copy(slot, f):
        return pltpu.make_async_copy(
            stage.at[slot], grad_h.at[:, pl.ds(pl.multiple_of(f * CH, CH), CH)], osem.at[slot]
        )

    def multiply(i):
        arrive(across[i])

        def step(t, carry):
            n = i * i + t
            slot = n % 2
            ga = xor2(a, mask_of(jnp.minimum(t, i)))
            gb = xor2(b, mask_of(jnp.minimum(i, 2 * i - t)))

            @pl.when(n >= 2)
            def _():
                out_copy(slot, 0).wait()

            stage[slot] = dot_nt(cot_v[...], wg[ga * 4 + gb]).astype(BF16)
            out_copy(slot, fid(ga, gb)).start()
            return carry

        lax.fori_loop(0, 2 * i + 1, step, 0)

    cot_sent = send(cot_h, cotp, at(aA, b))
    w_load.wait()
    own = wslice(a * 4 + b, 1, x, c)
    w_a = send(own, own, at(a, bA))
    w_b = send(own, own, at(a, bB))

    cot_load.wait()
    seed32 = stack(seed_ref[...])
    q32 = stack(fold(dot_nt(seed32, cot_v[...])))
    pltpu.make_async_copy(ctx_v, ctx_v, lsem.at[1]).wait()

    def left_terms(s, carry):
        even = fold(dot_nn(q32, ctx_v[2 * s]))
        odd = fold(dot_nn(q32, ctx_v[2 * s + 1]))
        ppart[s] = jnp.where(row8 < 4, even, odd) * SCALE
        return carry

    lax.fori_loop(0, N_DP, left_terms, 0)
    err_load.wait()
    err_term = fold(dot_nt(seed32, err_v[...]))
    mine8 = (row8 // 4) == (fs % 2)
    ppart[fs // 2] = ppart[fs // 2] + jnp.where(mine8, err_term, 0.0)

    rb1[dp] = ppart[dp]
    ph1 = dp_exchange(lambda peer: ppart.at[peer], rb1)
    w_a.wait_recv()
    src = wslice(a * 4 + bA, 1, x, c)
    w_f = send(src, src, at(a, bB))
    w_b.wait_recv()
    arrive(ph1)
    rb2[z] = total(rb1, N_DP)
    ph2 = z_exchange(rb2)

    send_columns(0)
    w_f.wait_recv()
    src = wslice(a * 4, 4, x, c)
    g_b = send(src, src, at(aB, b))
    x_own(0, 0)
    arrive(ph2)
    rb3[y] = total(rb2, 4)
    ph3 = y_exchange(rb3)

    send_columns(1)
    x_own(0, 1)
    arrive(ph3)
    pall[dp] = total(rb3, 4)
    ph4 = dp_exchange(lambda peer: pall.at[dp], pall)

    send_columns(2)
    cot_sent.wait_recv()
    make_first(0)
    send_first(0, 0)
    x_forward(0)
    send_first(0, 1)
    arrive(ph4)

    send_columns(3)
    g_b.wait_recv()
    x_own(1, 0)

    def inner(u, v):
        t = u[0] * v[0] + u[1] * v[1]
        return jnp.sum(jnp.sum(t, axis=1, keepdims=True), axis=0, keepdims=True)

    basis = []
    for j in range(4):
        v = (pall[:, j, :], pall[:, j + 4, :])
        if j:
            coeffs = [inner(q, v) for q in basis]
            cut0 = coeffs[0] * basis[0][0]
            cut1 = coeffs[0] * basis[0][1]
            for k in range(1, j):
                cut0 = cut0 + coeffs[k] * basis[k][0]
                cut1 = cut1 + coeffs[k] * basis[k][1]
            v = (v[0] - cut0, v[1] - cut1)
        length = jnp.sqrt(inner(v, v) + EPSILON)
        v = (v[0] / length, v[1] / length)
        basis.append(v)
        phat[:, j, :] = v[0]
        phat[:, j + 4, :] = v[1]

    def rows_terms(s, carry):
        p32 = stack(phat[s])
        return carry[0] + dot_nt(p32, ctx_v[2 * s]), carry[1] + dot_nt(p32, ctx_v[2 * s + 1])

    zero = jnp.zeros((32, TOK), F32)
    even, odd = lax.fori_loop(0, N_DP, rows_terms, (zero, zero))
    mix = jnp.where(row8 < 4, fold(even), fold(odd))
    h8 = mix + jnp.concatenate([mix[4:8], mix[0:4]], axis=0)
    slot_rows = phat[fs // 2]
    turned = jnp.concatenate([slot_rows[4:8], slot_rows[0:4]], axis=0)
    p8 = jnp.where(mine8, slot_rows, turned)
    r8 = fold(dot_nn(stack(h8), cot_v[...])) * SCALE + fold(dot_nn(stack(p8), err_v[...]))
    rb5[dp] = jnp.where(row8 < 4, r8[:, 0:512], r8[:, 512:1024])
    ph5 = dp_exchange(lambda peer: rb5.at[dp], rb5)

    make_first(1)
    send_first(1, 0)
    send_columns(4)
    x_own(1, 1)
    arrive(ph5)
    rb6[z] = total(rb5, N_DP)
    ph6 = z_exchange(rb6)

    send_first(1, 1)
    send_columns(5)
    make_second(0)
    opp_low = send(rsend.at[0, low], opp.at[0], at(a, bP))
    opp_high = send(rsend.at[0, high], opp.at[1], at(a, bM))
    x_forward(1)
    arrive(ph6)
    rb7[y] = total(rb6, 4)
    ph7 = y_exchange(rb7)

    src = wslice(a * 4, 4, x, c)
    g_a = send(src, src, at(aA, b))
    make_first(2)
    send_first(2, 0)
    send_columns(6)
    arrive(ph7)
    factor = total(rb7, 4) * (1.0 / N_DP)
    right_ref[:, 0:512] = factor[0:4]
    right_ref[:, 512:1024] = factor[4:8]
    send_first(2, 1)
    send_columns(7)
    ph, pm, plo = parts(p8)
    rh, rm, rl = parts(factor)
    lhs = jnp.concatenate([ph, ph, pm, ph, plo, pm], axis=0).astype(BF16)
    rhs = jnp.concatenate([rh, rm, rh, rl, rh, rm], axis=0)
    row48 = lax.broadcasted_iota(jnp.int32, rhs.shape, 0) % 8
    rhs = jnp.concatenate([jnp.where(row48 < 4, rhs, 0.0), jnp.where(row48 >= 4, rhs, 0.0)], axis=1).astype(BF16)
    base[...] = err_v[...].astype(F32) - dot_tn(lhs, rhs)

    make_second(1)
    direct_r = send(rsend.at[1, high], fin.at[0, high], at(a, bP))
    g_a.wait_recv()
    src = wslice(aA * 4, 4, x, c)
    g_f = send(src, src, at(aB, b))
    x_own(2, 0)
    x_own(2, 1)
    make_first(3)
    send_first(3, 0)
    send_first(3, 1)
    opp_low.wait_recv()
    rsend[1, low] = (rsend[1, low].astype(F32) + opp[0].astype(F32)).astype(BF16)
    through_r = send(rsend.at[1, low], fin.at[0, low], at(a, bP))
    x_finish(0)
    multiply(0)
    make_second(2)
    direct_l = send(rsend.at[2, low], fin.at[1, low], at(a, bM))
    opp_high.wait_recv()
    rsend[2, high] = (rsend[2, high].astype(F32) + opp[1].astype(F32)).astype(BF16)
    through_l = send(rsend.at[2, high], fin.at[1, high], at(a, bM))
    g_f.wait_recv()
    x_own(3, 0)
    x_own(3, 1)
    x_finish(1)
    x_forward(2)
    exchange[7].wait_recv()
    base[...] += product(fid(a, b), 7) * SCALE
    multiply(1)
    x_finish(2)
    x_forward(3)
    multiply(2)

    for half, rows, copies in (
        (0, low, (first[3, 0], through_r, direct_l)),
        (1, high, (first[3, 1], direct_r, through_l)),
    ):
        arrive(copies)
        gathered = s1r[3, rows].astype(F32) + (fin[0, rows].astype(F32) + fin[1, rows].astype(F32))
        newmem_ref[rows, :] = (base[rows, :] + gathered * SCALE).astype(BF16)

    x_finish(3)
    multiply(3)
    out_copy(0, 0).wait()
    out_copy(1, 0).wait()
    for copy in sent:
        copy.wait_send()


N_SEMS = 160


def shards(context, cotangent, out_weight, error_memory, seed_factor):
    vmem, hbm = pl.BlockSpec(memory_space=pltpu.VMEM), pl.BlockSpec(memory_space=pl.ANY)
    seed8 = jnp.concatenate([seed_factor, seed_factor], axis=0)
    small = pltpu.VMEM((8, 8, 512), F32)
    quad = pltpu.VMEM((4, 8, 512), F32)
    context_grad, new_memory, right_factor = pl.pallas_call(
        kernel,
        out_shape=(
            jax.ShapeDtypeStruct((TOK, CH * N_FSDP), BF16),
            jax.ShapeDtypeStruct((CH, D), BF16),
            jax.ShapeDtypeStruct((4, D), F32),
        ),
        in_specs=[vmem, hbm, hbm, hbm, hbm],
        out_specs=(hbm, vmem, vmem),
        scratch_shapes=[
            pltpu.VMEM((N_FSDP, TOK, CH), BF16),
            pltpu.VMEM((TOK, D), BF16),
            pltpu.VMEM((CH, D), BF16),
            pltpu.VMEM((TOK, D), BF16),
            pltpu.VMEM((8, TOK, CH), BF16),
            pltpu.VMEM((4, CH, D), BF16),
            pltpu.VMEM((4, CH, D), BF16),
            pltpu.VMEM((3, CH, D), BF16),
            pltpu.VMEM((2, 256, D), BF16),
            pltpu.VMEM((2, CH, D), BF16),
            pltpu.VMEM((N_FSDP, CH, D), BF16),
            pltpu.VMEM((2, TOK, CH), BF16),
            pltpu.VMEM((CH, D), F32),
            small, small, quad, quad, small, small, small, quad, quad,
            pltpu.SemaphoreType.DMA((4,)),
            pltpu.SemaphoreType.DMA((2,)),
            pltpu.SemaphoreType.DMA((N_SEMS,)),
            pltpu.SemaphoreType.DMA((N_SEMS,)),
        ],
        compiler_params=pltpu.CompilerParams(
            collective_id=0, has_side_effects=True, vmem_limit_bytes=60 * 2**20
        ),
        cost_estimate=pl.CostEstimate(flops=18 * 2**30, bytes_accessed=20 * 2**20, transcendentals=0),
        name="projection_gradient",
    )(seed8, cotangent, context, out_weight, error_memory[0])
    return context_grad, new_memory[None], right_factor


def solution(mesh):
    placed = (
        P(("dp", "fsdp"), None),
        P(("dp", "fsdp"), None),
        P("fsdp", None),
        P("dp", "fsdp", None),
        P(),
    )
    return jax.shard_map(
        shards,
        mesh=mesh,
        in_specs=placed,
        out_specs=(P(("dp", "fsdp"), None), P("dp", "fsdp", None), P()),
        check_vma=False,
    )
```

time: 529 us -> 143 us (0.27)
  blocking collectives: 339 us -> 0 us
  Pallas kernels: 0 us -> 131 us
  waiting for transfers between devices: 114 us -> 0 us
  matrix products: 53.9 us -> 0 us
  between operations: 16.9 us -> 0.66 us
  local copies, waits for them, and re-layouts: 1.19 us -> 9.44 us
    psum x9 -> x0, blocking collectives: 339 us -> none  [the longest x4 126 us: shards(): squared = lax.psum(jnp.sum(vector * vector), 'fsdp')]
    pallas_call x0 -> x1, Pallas kernels: none -> 131 us  [shards(): pl.pallas_call(kernel, out_shape=(jax.ShapeDtypeStruct((TOK, CH * N_FSDP)...]
    reduce_scatter x1 -> x0, waiting for transfers between devices: 113 us -> none  [shards(): lax.psum_scatter(lax.dot_general(context, cotangent, (((0,), (0,)), ((),...]
    dot_general x9 -> x0, matrix products: 53.9 us -> none  [the longest x1 29.7 us: shards(): lax.dot_general(cotangent, lax.all_gather(out_weight, 'fsdp', axis=0, til...]
    unnamed x10 -> x7, local copies, waits for them, and re-layouts: 1.19 us -> 9.44 us
  transfers between devices with their start and end apart: 2 -> 0, of which waited for: 1 -> 0; matrix products, arithmetic and copies ran while one was open for 1% -> 0% of each run, Pallas kernels for 0% -> 0%
where the time goes in v1:
time: 143 us
  Pallas kernels  131 us (92%)
  local copies, waits for them, and re-layouts  9.44 us (7%)
    pallas_call x1, Pallas kernels, shards(): pl.pallas_call(kernel, out_shape=(jax.ShapeDtypeStruct((TOK, CH * N_FSDP)...  131 us
    unnamed x7, local copies, waits for them, and re-layouts  9.44 us

profile of v1, /device:TPU:1, one launch (start us, length us, event | category | flops | bytes accessed | tf_op | source)
XLA Modules:
  0.0 142.6 jit_solution(11344155689094186999)
XLA Ops:
  0.6 1.4 pad_maximum_fusion.seed_ref
  2.0 131.1 %projection_gradient.1 = (bf16[512,8192]{1,0:T(8,128)(2,1)}, bf16[512,1024]{1,0:T(8,128)(2,1)}, f32[4,1024]{1,0:T(4,128)}) custom-call(f32[8,1024]{1,0:T(8,128)} %pad_maximum_fusion.seed_ref, bf16[512,1024]{1,0:T(8,128)(2,1)} %cot_h.1, bf16[512,8192]{1,0:T(8,128)(2,1)} %ctx_h.1, bf16[512,1024]{1,0:T(8,128)(2,1)} %w_h.1, bf16[512,1024]{1,0:T(8,128)(2,1)} %bitcast.3), custom_call_target="tpu_custom_call" | custom-call | flops 19327352832 | bytes 20971520 | tf_op jit(solution)/shard_map/projection_gradient/pallas_call | solution.py:413
  133.2 0.0 copy-start
  133.2 0.0 copy-start.1
  133.2 7.9 %copy.11 = bf16[512,8192]{1,0:T(8,128)(2,1)} copy(bf16[512,8192]{1,0:T(8,128)(2,1)} %get-tuple-element.12) | data formatting | bytes 16777216
  141.0 0.0 copy-done
  141.0 1.0 copy.12
  142.0 0.0 copy-done.1
  142.0 0.6 copy.13
Async XLA Ops:
  133.2 7.9 %copy-start = (bf16[512,1024]{1,0:T(8,128)(2,1)S(1)}, bf16[512,1024]{1,0:T(8,128)(2,1)}, u32[]{:S(2)}) copy-start(bf16[512,1024]{1,0:T(8,128)(2,1)} %get-tuple-element.7) | copy-start | bytes 3145732
  133.2 8.8 %copy-start.1 = (f32[4,1024]{1,0:T(4,128)S(1)}, f32[4,1024]{1,0:T(4,128)}, u32[]{:S(2)}) copy-start(f32[4,1024]{1,0:T(4,128)} %get-tuple-element.14) | copy-start | bytes 49156

commit v2 on v1

--- a/solution.py
+++ b/solution.py
@@ -61,10 +61,10 @@
 
 def kernel(
     seed_ref, cot_h, ctx_h, w_h, err_h,
-    grad_h, newmem_ref, right_ref,
-    ctx_v, cot_v, err_v, cotp, ctxp, s1s, s1r, rsend, opp, fin, wg, stage, base,
+    grad_ref, newmem_ref, right_ref,
+    ctx_v, cot_v, err_v, cotp, ctxp, s1s, s1r, rsend, opp, fin, wg, base,
     ppart, rb1, rb2, rb3, pall, phat, rb5, rb6, rb7,
-    lsem, osem, ssem, rsem,
+    lsem, ssem, rsem,
 ):
     dp, fs = lax.axis_index("dp"), lax.axis_index("fsdp")
     x, c = dp // 2, dp % 2
@@ -138,8 +138,8 @@
             t = t + buf[i]
         return t
 
-    def product(f, j):
-        return dot_tn(ctx_v[f], cot_v[...]) + dot_tn(ctxp[j], cotp[...])
+    def product(f, j, cols=slice(None)):
+        return dot_tn(ctx_v[f], cot_v[:, cols]) + dot_tn(ctxp[j], cotp[:, cols])
 
     exchange = {}
 
@@ -150,15 +150,12 @@
 
     first = {}
 
-    def make_first(k):
-        exchange[k].wait_recv()
-        s1s[k] = product(fid(aB, border[k]), k).astype(BF16)
-
-    def send_first(k, half):
-        rows = pl.ds(half * 256, 256)
-        first[k, half] = send(s1s.at[k, rows], s1r.at[k, rows], at(aB, b))
-
-    second = {}
+    def make_first(k, half):
+        if half == 0:
+            exchange[k].wait_recv()
+        cols = pl.ds(half * HALF, HALF)
+        s1s[k, :, cols] = product(fid(aB, border[k]), k, cols).astype(BF16)
+        first[k, half] = send(s1s.at[k, :, cols], s1r.at[k, :, cols], at(aB, b))
 
     def make_second(k):
         exchange[4 + k].wait_recv()
@@ -197,40 +194,43 @@
             send(wg.at[group(i) * 4 + j, :, my_cols], wg.at[j * 4 + group(i), :, my_cols], sibling) for j in range(4)
         ]
 
-    def out_copy(slot, f):
-        return pltpu.make_async_copy(
-            stage.at[slot], grad_h.at[:, pl.ds(pl.multiple_of(f * CH, CH), CH)], osem.at[slot]
-        )
-
     def multiply(i):
         arrive(across[i])
 
         def step(t, carry):
-            n = i * i + t
-            slot = n % 2
             ga = xor2(a, mask_of(jnp.minimum(t, i)))
             gb = xor2(b, mask_of(jnp.minimum(i, 2 * i - t)))
 
-            @pl.when(n >= 2)
-            def _():
-                out_copy(slot, 0).wait()
-
-            stage[slot] = dot_nt(cot_v[...], wg[ga * 4 + gb]).astype(BF16)
-            out_copy(slot, fid(ga, gb)).start()
+            cols = pl.ds(pl.multiple_of(fid(ga, gb) * CH, CH), CH)
+            grad_ref[:, cols] = dot_nt(cot_v[...], wg[ga * 4 + gb]).astype(BF16)
             return carry
 
         lax.fori_loop(0, 2 * i + 1, step, 0)
 
-    cot_sent = send(cot_h, cotp, at(aA, b))
+    def send_cotangent(half):
+        cols = pl.ds(half * HALF, HALF)
+        return send(cot_h.at[:, cols], cotp.at[:, cols], at(aA, b))
+
+    cot_low = send_cotangent(0)
     w_load.wait()
     own = wslice(a * 4 + b, 1, x, c)
     w_a = send(own, own, at(a, bA))
     w_b = send(own, own, at(a, bB))
-
     cot_load.wait()
-    seed32 = stack(seed_ref[...])
+    seed32 = stack(jnp.concatenate([seed_ref[...], seed_ref[...]], axis=0))
     q32 = stack(fold(dot_nt(seed32, cot_v[...])))
     pltpu.make_async_copy(ctx_v, ctx_v, lsem.at[1]).wait()
+    send_columns(0)
+    cot_high = send_cotangent(1)
+    w_a.wait_recv()
+    src = wslice(a * 4 + bA, 1, x, c)
+    w_f = send(src, src, at(a, bB))
+    w_b.wait_recv()
+    w_f.wait_recv()
+    src = wslice(a * 4, 4, x, c)
+    g_b = send(src, src, at(aB, b))
+    x_own(0, 0)
+    x_own(0, 1)
 
     def left_terms(s, carry):
         even = fold(dot_nn(q32, ctx_v[2 * s]))
@@ -246,40 +246,41 @@
 
     rb1[dp] = ppart[dp]
     ph1 = dp_exchange(lambda peer: ppart.at[peer], rb1)
-    w_a.wait_recv()
-    src = wslice(a * 4 + bA, 1, x, c)
-    w_f = send(src, src, at(a, bB))
-    w_b.wait_recv()
+
+    send_columns(1)
+    cot_low.wait_recv()
+    make_first(0, 0)
+    cot_high.wait_recv()
+    make_first(0, 1)
     arrive(ph1)
     rb2[z] = total(rb1, N_DP)
     ph2 = z_exchange(rb2)
-
-    send_columns(0)
-    w_f.wait_recv()
-    src = wslice(a * 4, 4, x, c)
-    g_b = send(src, src, at(aB, b))
-    x_own(0, 0)
+    g_b.wait_recv()
+    x_own(1, 0)
+    x_forward(0)
+    send_columns(2)
+    make_first(1, 0)
     arrive(ph2)
     rb3[y] = total(rb2, 4)
     ph3 = y_exchange(rb3)
 
-    send_columns(1)
-    x_own(0, 1)
+    send_columns(3)
+    make_first(1, 1)
     arrive(ph3)
     pall[dp] = total(rb3, 4)
     ph4 = dp_exchange(lambda peer: pall.at[dp], pall)
 
-    send_columns(2)
-    cot_sent.wait_recv()
-    make_first(0)
-    send_first(0, 0)
-    x_forward(0)
-    send_first(0, 1)
+    src = wslice(a * 4, 4, x, c)
+    g_a = send(src, src, at(aA, b))
+    x_own(1, 1)
+    make_second(0)
+    opp_low = send(rsend.at[0, low], opp.at[0], at(a, bP))
+    opp_high = send(rsend.at[0, high], opp.at[1], at(a, bM))
+    make_first(2, 0)
     arrive(ph4)
 
-    send_columns(3)
-    g_b.wait_recv()
-    x_own(1, 0)
+    send_columns(4)
+    x_forward(1)
 
     def inner(u, v):
         t = u[0] * v[0] + u[1] * v[1]
@@ -317,35 +318,39 @@
     rb5[dp] = jnp.where(row8 < 4, r8[:, 0:512], r8[:, 512:1024])
     ph5 = dp_exchange(lambda peer: rb5.at[dp], rb5)
 
-    make_first(1)
-    send_first(1, 0)
-    send_columns(4)
-    x_own(1, 1)
+    make_first(2, 1)
+    send_columns(5)
+    g_a.wait_recv()
+    src = wslice(aA * 4, 4, x, c)
+    g_f = send(src, src, at(aB, b))
+    x_own(2, 0)
     arrive(ph5)
     rb6[z] = total(rb5, N_DP)
     ph6 = z_exchange(rb6)
 
-    send_first(1, 1)
-    send_columns(5)
-    make_second(0)
-    opp_low = send(rsend.at[0, low], opp.at[0], at(a, bP))
-    opp_high = send(rsend.at[0, high], opp.at[1], at(a, bM))
-    x_forward(1)
+    send_columns(6)
+    x_own(2, 1)
+    make_second(1)
+    direct_r = send(rsend.at[1, high], fin.at[0, high], at(a, bP))
+    opp_low.wait_recv()
+    rsend[1, low] = (rsend[1, low].astype(F32) + opp[0].astype(F32)).astype(BF16)
+    through_r = send(rsend.at[1, low], fin.at[0, low], at(a, bP))
     arrive(ph6)
     rb7[y] = total(rb6, 4)
     ph7 = y_exchange(rb7)
 
-    src = wslice(a * 4, 4, x, c)
-    g_a = send(src, src, at(aA, b))
-    make_first(2)
-    send_first(2, 0)
-    send_columns(6)
+    send_columns(7)
+    make_first(3, 0)
+    make_first(3, 1)
+    x_finish(0)
+    x_forward(2)
+    g_f.wait_recv()
+    x_own(3, 0)
+    x_own(3, 1)
     arrive(ph7)
     factor = total(rb7, 4) * (1.0 / N_DP)
     right_ref[:, 0:512] = factor[0:4]
     right_ref[:, 512:1024] = factor[4:8]
-    send_first(2, 1)
-    send_columns(7)
     ph, pm, plo = parts(p8)
     rh, rm, rl = parts(factor)
     lhs = jnp.concatenate([ph, ph, pm, ph, plo, pm], axis=0).astype(BF16)
@@ -354,31 +359,13 @@
     rhs = jnp.concatenate([jnp.where(row48 < 4, rhs, 0.0), jnp.where(row48 >= 4, rhs, 0.0)], axis=1).astype(BF16)
     base[...] = err_v[...].astype(F32) - dot_tn(lhs, rhs)
 
-    make_second(1)
-    direct_r = send(rsend.at[1, high], fin.at[0, high], at(a, bP))
-    g_a.wait_recv()
-    src = wslice(aA * 4, 4, x, c)
-    g_f = send(src, src, at(aB, b))
-    x_own(2, 0)
-    x_own(2, 1)
-    make_first(3)
-    send_first(3, 0)
-    send_first(3, 1)
-    opp_low.wait_recv()
-    rsend[1, low] = (rsend[1, low].astype(F32) + opp[0].astype(F32)).astype(BF16)
-    through_r = send(rsend.at[1, low], fin.at[0, low], at(a, bP))
-    x_finish(0)
     multiply(0)
     make_second(2)
     direct_l = send(rsend.at[2, low], fin.at[1, low], at(a, bM))
     opp_high.wait_recv()
     rsend[2, high] = (rsend[2, high].astype(F32) + opp[1].astype(F32)).astype(BF16)
     through_l = send(rsend.at[2, high], fin.at[1, high], at(a, bM))
-    g_f.wait_recv()
-    x_own(3, 0)
-    x_own(3, 1)
     x_finish(1)
-    x_forward(2)
     exchange[7].wait_recv()
     base[...] += product(fid(a, b), 7) * SCALE
     multiply(1)
@@ -387,8 +374,8 @@
     multiply(2)
 
     for half, rows, copies in (
-        (0, low, (first[3, 0], through_r, direct_l)),
-        (1, high, (first[3, 1], direct_r, through_l)),
+        (0, low, (first[3, 0], first[3, 1], through_r, direct_l)),
+        (1, high, (direct_r, through_l)),
     ):
         arrive(copies)
         gathered = s1r[3, rows].astype(F32) + (fin[0, rows].astype(F32) + fin[1, rows].astype(F32))
@@ -396,8 +383,6 @@
 
     x_finish(3)
     multiply(3)
-    out_copy(0, 0).wait()
-    out_copy(1, 0).wait()
     for copy in sent:
         copy.wait_send()
 
@@ -407,18 +392,17 @@
 
 def shards(context, cotangent, out_weight, error_memory, seed_factor):
     vmem, hbm = pl.BlockSpec(memory_space=pltpu.VMEM), pl.BlockSpec(memory_space=pl.ANY)
-    seed8 = jnp.concatenate([seed_factor, seed_factor], axis=0)
     small = pltpu.VMEM((8, 8, 512), F32)
     quad = pltpu.VMEM((4, 8, 512), F32)
     context_grad, new_memory, right_factor = pl.pallas_call(
         kernel,
         out_shape=(
-            jax.ShapeDtypeStruct((TOK, CH * N_FSDP), BF16),
-            jax.ShapeDtypeStruct((CH, D), BF16),
-            jax.ShapeDtypeStruct((4, D), F32),
+            pltpu.VMEM((TOK, CH * N_FSDP), BF16),
+            pltpu.VMEM((CH, D), BF16),
+            pltpu.VMEM((4, D), F32),
         ),
         in_specs=[vmem, hbm, hbm, hbm, hbm],
-        out_specs=(hbm, vmem, vmem),
+        out_specs=(vmem, vmem, vmem),
         scratch_shapes=[
             pltpu.VMEM((N_FSDP, TOK, CH), BF16),
             pltpu.VMEM((TOK, D), BF16),
@@ -431,20 +415,18 @@
             pltpu.VMEM((2, 256, D), BF16),
             pltpu.VMEM((2, CH, D), BF16),
             pltpu.VMEM((N_FSDP, CH, D), BF16),
-            pltpu.VMEM((2, TOK, CH), BF16),
             pltpu.VMEM((CH, D), F32),
             small, small, quad, quad, small, small, small, quad, quad,
             pltpu.SemaphoreType.DMA((4,)),
-            pltpu.SemaphoreType.DMA((2,)),
             pltpu.SemaphoreType.DMA((N_SEMS,)),
             pltpu.SemaphoreType.DMA((N_SEMS,)),
         ],
         compiler_params=pltpu.CompilerParams(
-            collective_id=0, has_side_effects=True, vmem_limit_bytes=60 * 2**20
+            collective_id=0, has_side_effects=True, vmem_limit_bytes=52 * 2**20
         ),
         cost_estimate=pl.CostEstimate(flops=18 * 2**30, bytes_accessed=20 * 2**20, transcendentals=0),
         name="projection_gradient",
-    )(seed8, cotangent, context, out_weight, error_memory[0])
+    )(seed_factor, cotangent, context, out_weight, error_memory[0])
     return context_grad, new_memory[None], right_factor
 
 

time: 143 us -> 129 us (0.902)
  Pallas kernels: 131 us -> 123 us
  local copies, waits for them, and re-layouts: 9.44 us -> 4.97 us
    pallas_call x1, Pallas kernels: 131 us -> 123 us  [shards(): pl.pallas_call(kernel, out_shape=(pltpu.VMEM((TOK, CH * N_FSDP), BF16), p...]
    unnamed x7 -> x3, local copies, waits for them, and re-layouts: 9.44 us -> 4.97 us
where the time goes in v2:
time: 129 us; the launch traced here: 128 us
  Pallas kernels  123 us (95%)
  local copies, waits for them, and re-layouts  4.97 us (4%)
    pallas_call x1, Pallas kernels, shards(): pl.pallas_call(kernel, out_shape=(pltpu.VMEM((TOK, CH * N_FSDP), BF16), p...  123 us
    unnamed x3, local copies, waits for them, and re-layouts  4.97 us

profile of v2, /device:TPU:1, one launch (start us, length us, event | category | flops | bytes accessed | tf_op | source)
XLA Modules:
  0.0 128.1 jit_solution(14957506195833748502)
XLA Ops:
  0.6 122.5 %projection_gradient.1 = (bf16[512,8192]{1,0:T(8,128)(2,1)S(1)}, bf16[512,1024]{1,0:T(8,128)(2,1)S(1)}, f32[4,1024]{1,0:T(4,128)S(1)}) custom-call(f32[4,1024]{1,0:T(4,128)} %seed_ref.1, bf16[512,1024]{1,0:T(8,128)(2,1)} %cot_h.1, bf16[512,8192]{1,0:T(8,128)(2,1)} %ctx_h.1, bf16[512,1024]{1,0:T(8,128)(2,1)} %w_h.1, bf16[512,1024]{1,0:T(8,128)(2,1)} %bitcast.3), custom_call_target="tpu_custom_call" | custom-call | flops 19327352832 | bytes 20971520 | tf_op jit(solution)/shard_map/projection_gradient/pallas_call | solution.py:397
  123.2 3.4 %copy.11 = bf16[512,8192]{1,0:T(8,128)(2,1)} copy(bf16[512,8192]{1,0:T(8,128)(2,1)S(1)} %get-tuple-element.9) | data formatting | bytes 16777216
  126.6 1.0 copy.12
  127.5 0.6 copy.13

commit v3 on v0

v3 whole, which is shorter than its diff:
```python
import functools

import jax
import jax.numpy as jnp
import numpy as np
from jax import lax
from jax.experimental import pallas as pl
from jax.experimental.pallas import tpu as pltpu
from jax.sharding import PartitionSpec as P

MESH = pl.DeviceIdType.MESH
F32 = jnp.float32
BF16 = jnp.bfloat16
EPSILON = 1e-06
TOK = 512
CH = 512
D = 1024
N_DP = 8
N_FSDP = 16
PIECE = 128
HALF = 512
SCALE = float(np.float32(1.0) / np.sqrt(np.float32(TOK * N_FSDP)))
ORDER = (
    "w0", "E0", "q", "cot1", "P0", "wf", "xa", "P1", "ph1", "gb", "cot0", "x01", "m00", "ph2", "ga",
    "F01", "x10", "x11", "f0", "E4", "F00", "ph3", "ph4", "E2", "gf", "x20", "x21", "E1", "S0",
    "sb0", "f1", "GS", "h0", "F20", "F21", "E5", "h1", "h2", "ph5", "f2", "E3", "x30", "F10", "x31",
    "sb1", "m10", "F11", "E6", "m01", "ph6", "m11", "m21", "sb2", "m20", "ph7", "F30", "F31", "E7",
    "m02", "m12", "m22", "S2", "f3", "S1", "base0", "base1", "tl", "b70", "b71", "sb3", "tr", "m30",
    "m31", "m32", "m03", "m13", "m23", "m33", "fin0", "fin1",
)


def dot_tn(a, b):
    return lax.dot_general(a, b, (((0,), (0,)), ((), ())), preferred_element_type=F32)


def dot_nn(a, b):
    return lax.dot_general(a, b, (((1,), (0,)), ((), ())), preferred_element_type=F32)


def dot_nt(a, b):
    return lax.dot_general(a, b, (((1,), (1,)), ((), ())), preferred_element_type=F32)


def parts(v):
    hi = v.astype(BF16).astype(F32)
    rest = v - hi
    mid = rest.astype(BF16).astype(F32)
    return hi, mid, rest - mid


def stack(v):
    hi, mid, lo = parts(v)
    return jnp.concatenate([hi, mid, lo, jnp.zeros_like(hi)], axis=0).astype(BF16)


def fold(r):
    return r[0:8] + (r[8:16] + r[16:24])


def xor2(a, m):
    return ((a // 2 + m // 2) % 2) * 2 + (a % 2 + m % 2) % 2


def mask_of(i):
    return ((i + 1) % 3 + 1) * ((i + 2) // 3)


def kernel(
    seed_ref, cot_h, ctx_h, w_h, err_h,
    grad_ref, newmem_ref, right_ref,
    ctx_v, cot_v, err_v, cotp, ctxp, s1s, s1r, rsend, opp, fin, wg, base,
    ppart, rb1, rb2, rb3, pall, phat, rb5, rb6, rb7, hacc, p_own,
    lsem, ssem, rsem,
):
    dp, fs = lax.axis_index("dp"), lax.axis_index("fsdp")
    x, c = dp // 2, dp % 2
    z, y = fs // 4, fs % 4
    a, b = z * (1 - c) + y * c, y * (1 - c) + z * c

    def fid(i, j):
        return (i * (1 - c) + j * c) * 4 + j * (1 - c) + i * c

    def at(i, j):
        return (dp, fid(i, j))

    ga = [a, 3 - a, xor2(a, 1), xor2(a, 2)]
    gb = [b, 3 - b, xor2(b, 1), xor2(b, 2)]
    aB, aA, bB, bA = ga[1], ga[2], gb[1], gb[2]
    bP, bM = (b + 1) % 4, (b + 3) % 4
    xR, xL = (x + 1) % 4, (x + 3) % 4
    right_chip, left_chip = (xR * 2 + c, fs), (xL * 2 + c, fs)
    sibling = (x * 2 + 1 - c, fs)
    border = [(b + k) % 4 for k in (2, 1, 3, 0)]
    row8 = lax.broadcasted_iota(jnp.int32, (8, CH), 0)
    mine8 = (row8 // 4) == (fs % 2)
    low, high = pl.ds(0, 256), pl.ds(256, 256)
    halves = (pl.ds(0, HALF), pl.ds(HALF, HALF))

    loads = {}

    def load(name, src, dst):
        loads[name] = pltpu.make_async_copy(src, dst, lsem.at[len(loads)])
        loads[name].start()

    load("cot", cot_h, cot_v)
    load("w", w_h, wg.at[a * 4 + b])
    for f in range(N_FSDP):
        pltpu.make_async_copy(ctx_h.at[:, pl.ds(f * CH, CH)], ctx_v.at[f], lsem.at[3]).start()
    load("err", err_h, err_v)
    loads["ctx"] = pltpu.make_async_copy(ctx_v, ctx_v, lsem.at[3])

    barrier = pltpu.get_barrier_semaphore()
    peers = [((dp + i) % N_DP, fs) for i in range(1, N_DP)]
    peers += [at((a + i) % 4, b) for i in range(1, 4)]
    peers += [at(a, (b + i) % 4) for i in range(1, 4)]
    for peer in peers:
        pl.semaphore_signal(barrier, inc=1, device_id=peer, device_id_type=MESH)
    pl.semaphore_wait(barrier, len(peers))

    sent, flights, arrived = [], {}, set()

    def send(name, src, dst, device):
        n = len(sent)
        copy = pltpu.make_async_remote_copy(src, dst, ssem.at[n], rsem.at[n], device_id=device, device_id_type=MESH)
        copy.start()
        sent.append(copy)
        flights.setdefault(name, []).append(copy)

    def need(*names):
        for name in names:
            if name in loads:
                loads.pop(name).wait()
            elif name in flights and name not in arrived:
                arrived.add(name)
                for copy in flights[name]:
                    copy.wait_recv()
            else:
                assert name in arrived or name in ("cot", "w", "err", "ctx"), name

    def dp_exchange(name, src_of, buf):
        for i in range(1, N_DP):
            send(name, src_of((dp + i) % N_DP), buf.at[dp], ((dp + i) % N_DP, fs))

    def a_exchange(name, buf):
        for i in range(1, 4):
            send(name, buf.at[a], buf.at[a], at((a + i) % 4, b))

    def b_exchange(name, buf):
        for i in range(1, 4):
            send(name, buf.at[b], buf.at[b], at(a, (b + i) % 4))

    def total(buf, n):
        t = buf[0]
        for i in range(1, n):
            t = t + buf[i]
        return t

    def task_q():
        need("cot")
        seed32 = stack(jnp.concatenate([seed_ref[...], seed_ref[...]], axis=0))
        hacc[0] = dot_nt(seed32, cot_v[...])
        need("err")
        p_own[...] = jnp.where(mine8, fold(dot_nt(seed32, err_v[...])), 0.0)

    def left_terms(first, last):
        need("ctx")
        q32 = stack(fold(hacc[0]))

        def step(s, carry):
            even = fold(dot_nn(q32, ctx_v[2 * s]))
            odd = fold(dot_nn(q32, ctx_v[2 * s + 1]))
            ppart[s] = jnp.where(row8 < 4, even, odd) * SCALE
            return carry

        lax.fori_loop(first, last, step, 0)

    def task_P1():
        left_terms(4, 8)
        ppart[fs // 2] = ppart[fs // 2] + p_own[...]
        rb1[dp] = ppart[dp]

    def task_ph2():
        need("ph1")
        rb2[a] = total(rb1, N_DP)
        a_exchange("ph2", rb2)

    def task_ph3():
        need("ph2")
        rb3[b] = total(rb2, 4)
        b_exchange("ph3", rb3)

    def task_ph4():
        need("ph3")
        pall[dp] = total(rb3, 4)
        dp_exchange("ph4", lambda peer: pall.at[dp], pall)

    def inner(u, v):
        t = u[0] * v[0] + u[1] * v[1]
        return jnp.sum(jnp.sum(t, axis=1, keepdims=True), axis=0, keepdims=True)

    def task_GS():
        need("ph4")
        basis = []
        for j in range(4):
            v = (pall[:, j, :], pall[:, j + 4, :])
            if j:
                coeffs = [inner(q, v) for q in basis]
                cut0 = coeffs[0] * basis[0][0]
                cut1 = coeffs[0] * basis[0][1]
                for k in range(1, j):
                    cut0 = cut0 + coeffs[k] * basis[k][0]
                    cut1 = cut1 + coeffs[k] * basis[k][1]
                v = (v[0] - cut0, v[1] - cut1)
            length = jnp.sqrt(inner(v, v) + EPSILON)
            v = (v[0] / length, v[1] / length)
            basis.append(v)
            phat[:, j, :] = v[0]
            phat[:, j + 4, :] = v[1]

    def rows_terms(first, last):
        def step(s, carry):
            p32 = stack(phat[s])
            return carry[0] + dot_nt(p32, ctx_v[2 * s]), carry[1] + dot_nt(p32, ctx_v[2 * s + 1])

        return lax.fori_loop(first, last, step, (hacc[0], hacc[1]))

    def task_h0():
        hacc[...] = jnp.zeros_like(hacc)
        hacc[0], hacc[1] = rows_terms(0, 4)

    def task_h1():
        hacc[0], hacc[1] = rows_terms(4, 8)

    def task_h2():
        mix = jnp.where(row8 < 4, fold(hacc[0]), fold(hacc[1]))
        h8 = mix + jnp.concatenate([mix[4:8], mix[0:4]], axis=0)
        slot_rows = phat[fs // 2]
        turned = jnp.concatenate([slot_rows[4:8], slot_rows[0:4]], axis=0)
        p8 = jnp.where(mine8, slot_rows, turned)
        p_own[...] = p8
        r8 = fold(dot_nn(stack(h8), cot_v[...])) * SCALE + fold(dot_nn(stack(p8), err_v[...]))
        rb5[a] = jnp.where(row8 < 4, r8[:, 0:512], r8[:, 512:1024])

    def task_ph6():
        need("ph5")
        rb6[b] = total(rb5, 4)
        b_exchange("ph6", rb6)

    def task_ph7():
        need("ph6")
        rb7[dp] = total(rb6, 4)
        dp_exchange("ph7", lambda peer: rb7.at[dp], rb7)

    def approx(half, factor):
        ph, pm, plo = parts(p_own[...])
        rh, rm, rl = parts(jnp.where((row8 // 4) == half, factor, 0.0))
        lhs = jnp.concatenate([ph, ph, pm, ph, plo, pm], axis=0).astype(BF16)
        rhs = jnp.concatenate([rh, rm, rh, rl, rh, rm], axis=0).astype(BF16)
        base[:, halves[half]] = err_v[:, halves[half]].astype(F32) - dot_tn(lhs, rhs)

    def task_base0():
        need("ph7")
        factor = total(rb7, N_DP) * (1.0 / N_DP)
        hacc[0, 0:8] = factor
        right_ref[:, 0:512] = factor[0:4]
        right_ref[:, 512:1024] = factor[4:8]
        approx(0, factor)

    def task_cot(half):
        cols = halves[half]
        send(f"cot{half}", cot_h.at[:, cols], cotp.at[:, cols], at(aA, b))

    def task_E(j):
        need("ctx")
        send(f"E{j}", ctx_v.at[fid(3 - aA if j < 4 else aA, border[j % 4])], ctxp.at[j], at(aA, b))

    def product(f, j, cols=slice(None)):
        return dot_tn(ctx_v[f], cot_v[:, cols]) + dot_tn(ctxp[j], cotp[:, cols])

    def task_F(k, half):
        need("cot", f"E{k}", f"cot{half}")
        cols = halves[half]
        s1s[k, :, cols] = product(fid(aB, border[k]), k, cols).astype(BF16)
        send(f"F{k}{half}", s1s.at[k, :, cols], s1r.at[k, :, cols], at(aB, b))

    def task_S(k):
        need(f"E{4 + k}", f"F{k}0", f"F{k}1", "cot0", "cot1")
        rsend[k] = (product(fid(a, border[k]), 4 + k) + s1r[k].astype(F32)).astype(BF16)
        if k == 0:
            send("ol", rsend.at[0, low], opp.at[0], at(a, bP))
            send("oh", rsend.at[0, high], opp.at[1], at(a, bM))
        elif k == 1:
            send("dr", rsend.at[1, high], fin.at[0, high], at(a, bP))
        else:
            send("dl", rsend.at[2, low], fin.at[1, low], at(a, bM))

    def task_tr():
        need("ol")
        rsend[1, low] = (rsend[1, low].astype(F32) + opp[0].astype(F32)).astype(BF16)
        send("tr", rsend.at[1, low], fin.at[0, low], at(a, bP))

    def task_tl():
        need("oh")
        rsend[2, high] = (rsend[2, high].astype(F32) + opp[1].astype(F32)).astype(BF16)
        send("tl", rsend.at[2, high], fin.at[1, high], at(a, bM))

    def task_b7(half):
        need("E7", "cot0", "cot1")
        base[:, halves[half]] += product(fid(a, b), 7, halves[half]) * SCALE

    def task_fin(half):
        need("F30", "F31", *(("tr", "dl") if half == 0 else ("dr", "tl")))
        rows = (low, high)[half]
        gathered = s1r[3, rows].astype(F32) + (fin[0, rows].astype(F32) + fin[1, rows].astype(F32))
        newmem_ref[rows, :] = (base[rows, :] + gathered * SCALE).astype(BF16)

    def wslice(first, count, slot, rows=PIECE, shift=0):
        return wg.at[
            pl.ds(first, count),
            pl.ds(pl.multiple_of(slot * PIECE + shift, rows), rows),
            pl.ds(pl.multiple_of(c * HALF, HALF), HALF),
        ]

    def pass_on(name, src, device):
        send(name, src, src, device)

    def task_w0():
        need("w")
        pass_on("wa", wslice(a * 4 + b, 1, x), at(a, bA))
        pass_on("wb", wslice(a * 4 + b, 1, x), at(a, bB))

    def task_wf():
        need("wa")
        pass_on("wf", wslice(a * 4 + bA, 1, x), at(a, bB))

    def task_group(name, needed, source, target):
        need(*needed)
        pass_on(name, wslice(source * 4, 4, x), at(target, b))

    def both(name, first, count):
        pass_on(name + "r", wslice(first, count, x), right_chip)
        pass_on(name + "l", wslice(first, count, x), left_chip)

    def task_xa():
        need("wa")
        both("xa", a * 4 + bA, 1)

    other_pair = a * 4 + (1 - b // 2) * 2

    def task_x01():
        need("wb", "wf")
        both("x01", other_pair, 2)

    def task_x(i, part):
        need((None, "gb", "ga", "gf")[i])
        both(f"x{i}{part}", ga[i] * 4 + part * 2, 2)

    def task_f(i):
        if i == 0:
            need("xar", "xal", "x01r", "x01l")
            pass_on("f0", wslice(a * 4 + bA, 1, xL, 64, 0), right_chip)
            pass_on("f0", wslice(a * 4 + bA, 1, xR, 64, 64), left_chip)
            pass_on("f0", wslice(other_pair, 1, xL), right_chip)
            pass_on("f0", wslice(other_pair + 1, 1, xR), left_chip)
        else:
            need(f"x{i}0r", f"x{i}1l")
            pass_on(f"f{i}", wslice(ga[i] * 4, 2, xL), right_chip)
            pass_on(f"f{i}", wslice(ga[i] * 4 + 2, 2, xR), left_chip)

    def ring_done(i):
        if i:
            need(f"x{i}0r", f"x{i}1l", f"x{i}0l", f"x{i}1r", f"f{i}")
        else:
            need("xar", "xal", "x01r", "x01l", "f0")

    def task_sb(i):
        ring_done(i)
        cols = pl.ds(pl.multiple_of(c * HALF, HALF), HALF)
        for u in range(4):
            if i + u:
                send(f"sb{i}{u}", wg.at[ga[i] * 4 + gb[u], :, cols], wg.at[gb[u] * 4 + ga[i], :, cols], sibling)

    def task_m(i, u):
        need("cot")
        if i + u:
            ring_done(i)
            need(f"sb{u}{i}")
        else:
            need("w")
        cols = pl.ds(pl.multiple_of(fid(ga[i], gb[u]) * CH, CH), CH)
        grad_ref[:, cols] = dot_nt(cot_v[...], wg[ga[i] * 4 + gb[u]]).astype(BF16)

    tasks = {
        "w0": task_w0, "wf": task_wf, "xa": task_xa, "x01": task_x01,
        "gb": functools.partial(task_group, "gb", ("wa", "wb", "wf"), a, aB),
        "ga": functools.partial(task_group, "ga", ("wa", "wb", "wf"), a, aA),
        "gf": functools.partial(task_group, "gf", ("ga",), aA, aB),
        "q": task_q, "P0": functools.partial(left_terms, 0, 4), "P1": task_P1,
        "ph1": functools.partial(dp_exchange, "ph1", lambda peer: ppart.at[peer], rb1),
        "ph2": task_ph2, "ph3": task_ph3, "ph4": task_ph4,
        "GS": task_GS, "h0": task_h0, "h1": task_h1, "h2": task_h2,
        "ph5": functools.partial(a_exchange, "ph5", rb5), "ph6": task_ph6, "ph7": task_ph7,
        "base0": task_base0, "base1": lambda: approx(1, hacc[0, 0:8]),
        "tr": task_tr, "tl": task_tl,
    }
    for i in range(8):
        tasks[f"E{i}"] = functools.partial(task_E, i)
    for i in range(4):
        tasks[f"f{i}"] = functools.partial(task_f, i)
        tasks[f"sb{i}"] = functools.partial(task_sb, i)
        if i < 3:
            tasks[f"S{i}"] = functools.partial(task_S, i)
        for u in range(4):
            tasks[f"m{i}{u}"] = functools.partial(task_m, i, u)
        for u in range(2):
            tasks[f"F{i}{u}"] = functools.partial(task_F, i, u)
            if i:
                tasks[f"x{i}{u}"] = functools.partial(task_x, i, u)
    for u in range(2):
        tasks[f"cot{u}"] = functools.partial(task_cot, u)
        tasks[f"b7{u}"] = functools.partial(task_b7, u)
        tasks[f"fin{u}"] = functools.partial(task_fin, u)

    assert sorted(ORDER) == sorted(tasks)
    for name in ORDER:
        tasks[name]()

    need(*(name for name in flights))
    for copy in sent:
        copy.wait_send()


N_SEMS = 160


def shards(context, cotangent, out_weight, error_memory, seed_factor):
    vmem, hbm = pl.BlockSpec(memory_space=pltpu.VMEM), pl.BlockSpec(memory_space=pl.ANY)
    small = pltpu.VMEM((8, 8, 512), F32)
    quad = pltpu.VMEM((4, 8, 512), F32)
    context_grad, new_memory, right_factor = pl.pallas_call(
        kernel,
        out_shape=(
            pltpu.VMEM((TOK, CH * N_FSDP), BF16),
            pltpu.VMEM((CH, D), BF16),
            pltpu.VMEM((4, D), F32),
        ),
        in_specs=[vmem, hbm, hbm, hbm, hbm],
        out_specs=(vmem, vmem, vmem),
        scratch_shapes=[
            pltpu.VMEM((N_FSDP, TOK, CH), BF16),
            pltpu.VMEM((TOK, D), BF16),
            pltpu.VMEM((CH, D), BF16),
            pltpu.VMEM((TOK, D), BF16),
            pltpu.VMEM((8, TOK, CH), BF16),
            pltpu.VMEM((4, CH, D), BF16),
            pltpu.VMEM((4, CH, D), BF16),
            pltpu.VMEM((3, CH, D), BF16),
            pltpu.VMEM((2, 256, D), BF16),
            pltpu.VMEM((2, CH, D), BF16),
            pltpu.VMEM((N_FSDP, CH, D), BF16),
            pltpu.VMEM((CH, D), F32),
            small, small, quad, quad, small, small, quad, quad, small,
            pltpu.VMEM((2, 32, TOK), F32),
            pltpu.VMEM((8, CH), F32),
            pltpu.SemaphoreType.DMA((4,)),
            pltpu.SemaphoreType.DMA((N_SEMS,)),
            pltpu.SemaphoreType.DMA((N_SEMS,)),
        ],
        compiler_params=pltpu.CompilerParams(
            collective_id=0, has_side_effects=True, vmem_limit_bytes=52 * 2**20
        ),
        cost_estimate=pl.CostEstimate(flops=18 * 2**30, bytes_accessed=20 * 2**20, transcendentals=0),
        name="projection_gradient",
    )(seed_factor, cotangent, context, out_weight, error_memory[0])
    return context_grad, new_memory[None], right_factor


def solution(mesh):
    placed = (
        P(("dp", "fsdp"), None),
        P(("dp", "fsdp"), None),
        P("fsdp", None),
        P("dp", "fsdp", None),
        P(),
    )
    return jax.shard_map(
        shards,
        mesh=mesh,
        in_specs=placed,
        out_specs=(P(("dp", "fsdp"), None), P("dp", "fsdp", None), P()),
        check_vma=False,
    )
```

time: 529 us -> 108 us (0.20)
  blocking collectives: 339 us -> 0 us
  waiting for transfers between devices: 114 us -> 0 us
  Pallas kernels: 0 us -> 103 us
  matrix products: 53.9 us -> 0 us
  between operations: 16.9 us -> 0.64 us
    psum x9 -> x0, blocking collectives: 339 us -> none  [the longest x4 126 us: shards(): squared = lax.psum(jnp.sum(vector * vector), 'fsdp')]
    reduce_scatter x1 -> x0, waiting for transfers between devices: 113 us -> none  [shards(): lax.psum_scatter(lax.dot_general(context, cotangent, (((0,), (0,)), ((),...]
    pallas_call x0 -> x1, Pallas kernels: none -> 103 us  [shards(): pl.pallas_call(kernel, out_shape=(pltpu.VMEM((TOK, CH * N_FSDP), BF16), p...]
    dot_general x9 -> x0, matrix products: 53.9 us -> none  [the longest x1 29.7 us: shards(): lax.dot_general(cotangent, lax.all_gather(out_weight, 'fsdp', axis=0, til...]
  transfers between devices with their start and end apart: 2 -> 0, of which waited for: 1 -> 0; matrix products, arithmetic and copies ran while one was open for 1% -> 0% of each run, Pallas kernels for 0% -> 0%
where the time goes in v3:
time: 108 us
  Pallas kernels  103 us (95%)
  local copies, waits for them, and re-layouts  4.97 us (5%)
    pallas_call x1, Pallas kernels, shards(): pl.pallas_call(kernel, out_shape=(pltpu.VMEM((TOK, CH * N_FSDP), BF16), p...  103 us
    unnamed x3, local copies, waits for them, and re-layouts  4.97 us

profile of v3, /device:TPU:1, one launch (start us, length us, event | category | flops | bytes accessed | tf_op | source)
XLA Modules:
  0.0 108.1 jit_solution(17256022522760490692)
XLA Ops:
  0.6 102.5 %projection_gradient.1 = (bf16[512,8192]{1,0:T(8,128)(2,1)S(1)}, bf16[512,1024]{1,0:T(8,128)(2,1)S(1)}, f32[4,1024]{1,0:T(4,128)S(1)}) custom-call(f32[4,1024]{1,0:T(4,128)} %seed_ref.1, bf16[512,1024]{1,0:T(8,128)(2,1)} %cot_h.1, bf16[512,8192]{1,0:T(8,128)(2,1)} %ctx_h.1, bf16[512,1024]{1,0:T(8,128)(2,1)} %w_h.1, bf16[512,1024]{1,0:T(8,128)(2,1)} %bitcast.3), custom_call_target="tpu_custom_call" | custom-call | flops 19327352832 | bytes 20971520 | tf_op jit(solution)/shard_map/projection_gradient/pallas_call | solution.py:441
  103.2 3.4 %copy.11 = bf16[512,8192]{1,0:T(8,128)(2,1)} copy(bf16[512,8192]{1,0:T(8,128)(2,1)S(1)} %get-tuple-element.9) | data formatting | bytes 16777216
  106.6 1.0 copy.12
  107.5 0.6 copy.13

commit v4 on v3

--- a/solution.py
+++ b/solution.py
@@ -20,13 +20,15 @@
 PIECE = 128
 HALF = 512
 SCALE = float(np.float32(1.0) / np.sqrt(np.float32(TOK * N_FSDP)))
+CUT = 256
 ORDER = (
-    "w0", "E0", "q", "cot1", "P0", "wf", "xa", "P1", "ph1", "gb", "cot0", "x01", "m00", "ph2", "ga",
-    "F01", "x10", "x11", "f0", "E4", "F00", "ph3", "ph4", "E2", "gf", "x20", "x21", "E1", "S0",
-    "sb0", "f1", "GS", "h0", "F20", "F21", "E5", "h1", "h2", "ph5", "f2", "E3", "x30", "F10", "x31",
-    "sb1", "m10", "F11", "E6", "m01", "ph6", "m11", "m21", "sb2", "m20", "ph7", "F30", "F31", "E7",
-    "m02", "m12", "m22", "S2", "f3", "S1", "base0", "base1", "tl", "b70", "b71", "sb3", "tr", "m30",
-    "m31", "m32", "m03", "m13", "m23", "m33", "fin0", "fin1",
+    "w0", "q", "E1", "cot1", "gB0", "P0", "E0b", "xa", "wf", "P1", "ph1", "gB1", "x01", "gB2",
+    "m00", "ph2", "E0", "ga", "cot0", "x10", "F11", "x11", "ph3", "F01", "ph4", "cot0b", "gf",
+    "x20", "E2", "x21", "F00", "GS", "E4", "f1", "F10", "h0", "F00b", "f0", "h1", "h2", "F00c",
+    "f2", "ph5", "E3", "E6", "F21", "sb1", "S0", "F30", "x30", "sb0", "E5", "ph6", "m01", "F20",
+    "m11", "x31", "sb2", "F31", "E7", "m20", "m10", "m12", "m22", "m02", "m21", "ph7", "f3", "S1",
+    "tA", "S2", "tB", "base0", "base1", "sb3", "m31", "m32", "b70", "m30", "m13", "b71", "m23",
+    "m33", "fin0", "m03", "fin1",
 )
 
 
@@ -87,16 +89,21 @@
     ga = [a, 3 - a, xor2(a, 1), xor2(a, 2)]
     gb = [b, 3 - b, xor2(b, 1), xor2(b, 2)]
     aB, aA, bB, bA = ga[1], ga[2], gb[1], gb[2]
-    bP, bM = (b + 1) % 4, (b + 3) % 4
     xR, xL = (x + 1) % 4, (x + 3) % 4
     right_chip, left_chip = (xR * 2 + c, fs), (xL * 2 + c, fs)
     sibling = (x * 2 + 1 - c, fs)
-    border = [(b + k) % 4 for k in (2, 1, 3, 0)]
+    border = [gb[3], bA, bB, b]
     row8 = lax.broadcasted_iota(jnp.int32, (8, CH), 0)
     mine8 = (row8 // 4) == (fs % 2)
-    low, high = pl.ds(0, 256), pl.ds(256, 256)
+    low, high = pl.ds(0, CUT), pl.ds(CUT, CH - CUT)
     halves = (pl.ds(0, HALF), pl.ds(HALF, HALF))
 
+    barrier = pltpu.get_barrier_semaphore()
+    peers = [((dp + i) % N_DP, fs) for i in range(1, N_DP)]
+    peers += [at((a + i) % 4, b) for i in range(1, 4)]
+    peers += [at(a, (b + i) % 4) for i in range(1, 4)]
+    for peer in peers:
+        pl.semaphore_signal(barrier, inc=1, device_id=peer, device_id_type=MESH)
     loads = {}
 
     def load(name, src, dst):
@@ -110,12 +117,6 @@
     load("err", err_h, err_v)
     loads["ctx"] = pltpu.make_async_copy(ctx_v, ctx_v, lsem.at[3])
 
-    barrier = pltpu.get_barrier_semaphore()
-    peers = [((dp + i) % N_DP, fs) for i in range(1, N_DP)]
-    peers += [at((a + i) % 4, b) for i in range(1, 4)]
-    peers += [at(a, (b + i) % 4) for i in range(1, 4)]
-    for peer in peers:
-        pl.semaphore_signal(barrier, inc=1, device_id=peer, device_id_type=MESH)
     pl.semaphore_wait(barrier, len(peers))
 
     sent, flights, arrived = [], {}, set()
@@ -267,50 +268,66 @@
         right_ref[:, 512:1024] = factor[4:8]
         approx(0, factor)
 
-    def task_cot(half):
-        cols = halves[half]
-        send(f"cot{half}", cot_h.at[:, cols], cotp.at[:, cols], at(aA, b))
+    def task_cot(name, first, count):
+        cols = pl.ds(first, count)
+        send(name, cot_h.at[:, cols], cotp.at[:, cols], at(aA, b))
+
+    quarters = (pl.ds(0, 256), pl.ds(256, 256))
 
     def task_E(j):
         need("ctx")
         send(f"E{j}", ctx_v.at[fid(3 - aA if j < 4 else aA, border[j % 4])], ctxp.at[j], at(aA, b))
 
-    def product(f, j, cols=slice(None)):
-        return dot_tn(ctx_v[f], cot_v[:, cols]) + dot_tn(ctxp[j], cotp[:, cols])
+    def task_E0(part):
+        need("ctx")
+        cols = quarters[part]
+        send(("E0", "E0b")[part], ctx_v.at[fid(3 - aA, border[0]), :, cols], ctxp.at[0, :, cols], at(aA, b))
+
+    def product(f, j, cols=slice(None), rows=slice(None)):
+        return dot_tn(ctx_v[f, :, rows], cot_v[:, cols]) + dot_tn(ctxp[j, :, rows], cotp[:, cols])
 
     def task_F(k, half):
-        need("cot", f"E{k}", f"cot{half}")
+        need("cot", f"E{k}", *(("cot0", "cot0b") if half == 0 else ("cot1",)))
+        if k == 0:
+            need("E0b")
         cols = halves[half]
         s1s[k, :, cols] = product(fid(aB, border[k]), k, cols).astype(BF16)
         send(f"F{k}{half}", s1s.at[k, :, cols], s1r.at[k, :, cols], at(aB, b))
 
+    def task_F0(name, needed, rows, cols):
+        need("cot", "cot0", *needed)
+        s1s[0, rows, cols] = product(fid(aB, border[0]), 0, cols, rows).astype(BF16)
+        send(name, s1s.at[0, rows, cols], s1r.at[0, rows, cols], at(aB, b))
+
     def task_S(k):
-        need(f"E{4 + k}", f"F{k}0", f"F{k}1", "cot0", "cot1")
+        need(f"E{4 + k}", f"F{k}0", f"F{k}1", "cot0", "cot0b", "cot1")
+        if k == 0:
+            need("F00b", "F00c")
         rsend[k] = (product(fid(a, border[k]), 4 + k) + s1r[k].astype(F32)).astype(BF16)
         if k == 0:
-            send("ol", rsend.at[0, low], opp.at[0], at(a, bP))
-            send("oh", rsend.at[0, high], opp.at[1], at(a, bM))
+            send("oB", rsend.at[0, low], opp.at[0], at(a, bB))
+            send("oA", rsend.at[0, high], opp.at[1, pl.ds(0, CH - CUT)], at(a, bA))
         elif k == 1:
-            send("dr", rsend.at[1, high], fin.at[0, high], at(a, bP))
+            send("dA", rsend.at[1, high], fin.at[0, high], at(a, bA))
         else:
-            send("dl", rsend.at[2, low], fin.at[1, low], at(a, bM))
-
-    def task_tr():
-        need("ol")
+            send("dB", rsend.at[2, low], fin.at[1, low], at(a, bB))
+
+    def task_tA():
+        need("oB")
         rsend[1, low] = (rsend[1, low].astype(F32) + opp[0].astype(F32)).astype(BF16)
-        send("tr", rsend.at[1, low], fin.at[0, low], at(a, bP))
-
-    def task_tl():
-        need("oh")
-        rsend[2, high] = (rsend[2, high].astype(F32) + opp[1].astype(F32)).astype(BF16)
-        send("tl", rsend.at[2, high], fin.at[1, high], at(a, bM))
+        send("tA", rsend.at[1, low], fin.at[0, low], at(a, bA))
+
+    def task_tB():
+        need("oA")
+        rsend[2, high] = (rsend[2, high].astype(F32) + opp[1, 0:CH - CUT].astype(F32)).astype(BF16)
+        send("tB", rsend.at[2, high], fin.at[1, high], at(a, bB))
 
     def task_b7(half):
-        need("E7", "cot0", "cot1")
+        need("E7", "cot0", "cot0b", "cot1")
         base[:, halves[half]] += product(fid(a, b), 7, halves[half]) * SCALE
 
     def task_fin(half):
-        need("F30", "F31", *(("tr", "dl") if half == 0 else ("dr", "tl")))
+        need("F30", "F31", *(("tA", "dB") if half == 0 else ("dA", "tB")))
         rows = (low, high)[half]
         gathered = s1r[3, rows].astype(F32) + (fin[0, rows].astype(F32) + fin[1, rows].astype(F32))
         newmem_ref[rows, :] = (base[rows, :] + gathered * SCALE).astype(BF16)
@@ -338,6 +355,10 @@
         need(*needed)
         pass_on(name, wslice(source * 4, 4, x), at(target, b))
 
+    def task_block(name, needed, first, count, target):
+        need(*needed)
+        pass_on(name, wslice(first, count, x), at(target, b))
+
     def both(name, first, count):
         pass_on(name + "r", wslice(first, count, x), right_chip)
         pass_on(name + "l", wslice(first, count, x), left_chip)
@@ -353,7 +374,7 @@
         both("x01", other_pair, 2)
 
     def task_x(i, part):
-        need((None, "gb", "ga", "gf")[i])
+        need(*((), ("gB0", "gB1", "gB2"), ("ga",), ("gf",))[i])
         both(f"x{i}{part}", ga[i] * 4 + part * 2, 2)
 
     def task_f(i):
@@ -393,7 +414,9 @@
 
     tasks = {
         "w0": task_w0, "wf": task_wf, "xa": task_xa, "x01": task_x01,
-        "gb": functools.partial(task_group, "gb", ("wa", "wb", "wf"), a, aB),
+        "gB0": functools.partial(task_block, "gB0", ("w",), a * 4 + b, 1, aB),
+        "gB1": functools.partial(task_block, "gB1", ("wa",), a * 4 + bA, 1, aB),
+        "gB2": functools.partial(task_block, "gB2", ("wb", "wf"), other_pair, 2, aB),
         "ga": functools.partial(task_group, "ga", ("wa", "wb", "wf"), a, aA),
         "gf": functools.partial(task_group, "gf", ("ga",), aA, aB),
         "q": task_q, "P0": functools.partial(left_terms, 0, 4), "P1": task_P1,
@@ -402,7 +425,13 @@
         "GS": task_GS, "h0": task_h0, "h1": task_h1, "h2": task_h2,
         "ph5": functools.partial(a_exchange, "ph5", rb5), "ph6": task_ph6, "ph7": task_ph7,
         "base0": task_base0, "base1": lambda: approx(1, hacc[0, 0:8]),
-        "tr": task_tr, "tl": task_tl,
+        "tA": task_tA, "tB": task_tB,
+        "E0b": functools.partial(task_E0, 1),
+        "F00b": functools.partial(task_F0, "F00b", ("cot0b", "E0"), quarters[0], quarters[1]),
+        "F00c": functools.partial(task_F0, "F00c", ("cot0b", "E0b"), quarters[1], halves[0]),
+        "cot0": functools.partial(task_cot, "cot0", 0, 256),
+        "cot0b": functools.partial(task_cot, "cot0b", 256, 256),
+        "cot1": functools.partial(task_cot, "cot1", 512, 512),
     }
     for i in range(8):
         tasks[f"E{i}"] = functools.partial(task_E, i)
@@ -418,17 +447,44 @@
             if i:
                 tasks[f"x{i}{u}"] = functools.partial(task_x, i, u)
     for u in range(2):
-        tasks[f"cot{u}"] = functools.partial(task_cot, u)
         tasks[f"b7{u}"] = functools.partial(task_b7, u)
         tasks[f"fin{u}"] = functools.partial(task_fin, u)
 
+    tasks["E0"] = functools.partial(task_E0, 0)
+    tasks["F00"] = functools.partial(task_F0, "F00", ("E0",), quarters[0], quarters[0])
+
     assert sorted(ORDER) == sorted(tasks)
-    for name in ORDER:
+    drained = 0
+    first_fin = min(ORDER.index("fin0"), ORDER.index("fin1"))
+    points = {ORDER.index("f3"): 40, ORDER.index("sb3"): 24, first_fin: 14}
+    for place, name in enumerate(ORDER):
+        if place in points:
+            until = max(drained, len(sent) - points[place])
+            for copy in sent[drained:until]:
+                copy.wait_send()
+            drained = until
         tasks[name]()
 
     need(*(name for name in flights))
-    for copy in sent:
+    for copy in sent[drained:]:
         copy.wait_send()
+
+
+N_WRITES = 4
+
+
+def write_out(grad_v, new_v, right_v, grad_h, new_h, right_h, sem):
+    rows = TOK // N_WRITES
+    copies = [
+        pltpu.make_async_copy(grad_v.at[pl.ds(i * rows, rows)], grad_h.at[pl.ds(i * rows, rows)], sem.at[i])
+        for i in range(N_WRITES)
+    ]
+    copies.append(pltpu.make_async_copy(new_v, new_h, sem.at[N_WRITES]))
+    copies.append(pltpu.make_async_copy(right_v, right_h, sem.at[N_WRITES + 1]))
+    for copy in copies:
+        copy.start()
+    for copy in copies:
+        copy.wait()
 
 
 N_SEMS = 160
@@ -438,7 +494,7 @@
     vmem, hbm = pl.BlockSpec(memory_space=pltpu.VMEM), pl.BlockSpec(memory_space=pl.ANY)
     small = pltpu.VMEM((8, 8, 512), F32)
     quad = pltpu.VMEM((4, 8, 512), F32)
-    context_grad, new_memory, right_factor = pl.pallas_call(
+    results = pl.pallas_call(
         kernel,
         out_shape=(
             pltpu.VMEM((TOK, CH * N_FSDP), BF16),
@@ -456,7 +512,7 @@
             pltpu.VMEM((4, CH, D), BF16),
             pltpu.VMEM((4, CH, D), BF16),
             pltpu.VMEM((3, CH, D), BF16),
-            pltpu.VMEM((2, 256, D), BF16),
+            pltpu.VMEM((2, CUT, D), BF16),
             pltpu.VMEM((2, CH, D), BF16),
             pltpu.VMEM((N_FSDP, CH, D), BF16),
             pltpu.VMEM((CH, D), F32),
@@ -473,6 +529,16 @@
         cost_estimate=pl.CostEstimate(flops=18 * 2**30, bytes_accessed=20 * 2**20, transcendentals=0),
         name="projection_gradient",
     )(seed_factor, cotangent, context, out_weight, error_memory[0])
+    context_grad, new_memory, right_factor = pl.pallas_call(
+        write_out,
+        out_shape=tuple(jax.ShapeDtypeStruct(r.shape, r.dtype) for r in results),
+        in_specs=[hbm] * 3,
+        out_specs=(hbm,) * 3,
+        scratch_shapes=[pltpu.SemaphoreType.DMA((N_WRITES + 2,))],
+        cost_estimate=pl.CostEstimate(flops=0, bytes_accessed=9 * 2**20, transcendentals=0),
+        compiler_params=pltpu.CompilerParams(vmem_limit_bytes=2**20),
+        name="write_out",
+    )(*(pltpu.with_memory_space_constraint(r, pltpu.VMEM) for r in results))
     return context_grad, new_memory[None], right_factor
 
 

time: 108 us -> 103 us (0.954)
  local copies, waits for them, and re-layouts: 4.97 us -> 0 us
    unnamed x3 -> x0, local copies, waits for them, and re-layouts: 4.97 us -> none
    pallas_call x1, Pallas kernels: 103 us -> 98.5 us  [shards(): pl.pallas_call(kernel, out_shape=(pltpu.VMEM((TOK, CH * N_FSDP), BF16), p...]
    pallas_call x0 -> x1, Pallas kernels: none -> 3.67 us  [shards(): pl.pallas_call(write_out, out_shape=tuple((jax.ShapeDtypeStruct(r.shape,...]
where the time goes in v4:
time: 103 us
  Pallas kernels  102 us (99%)
    pallas_call x1, Pallas kernels, shards(): pl.pallas_call(kernel, out_shape=(pltpu.VMEM((TOK, CH * N_FSDP), BF16), p...  98.5 us
    pallas_call x1, Pallas kernels, shards(): pl.pallas_call(write_out, out_shape=tuple((jax.ShapeDtypeStruct(r.shape,...  3.67 us

profile of v4, /device:TPU:1, one launch (start us, length us, event | category | flops | bytes accessed | tf_op | source)
XLA Modules:
  0.0 103.0 jit_solution(3637784750010939990)
XLA Ops:
  0.6 98.5 %projection_gradient.1 = (bf16[512,8192]{1,0:T(8,128)(2,1)S(1)}, bf16[512,1024]{1,0:T(8,128)(2,1)S(1)}, f32[4,1024]{1,0:T(4,128)S(1)}) custom-call(f32[4,1024]{1,0:T(4,128)} %seed_ref.1, bf16[512,1024]{1,0:T(8,128)(2,1)} %cot_h.1, bf16[512,8192]{1,0:T(8,128)(2,1)} %ctx_h.1, bf16[512,1024]{1,0:T(8,128)(2,1)} %w_h.1, bf16[512,1024]{1,0:T(8,128)(2,1)} %bitcast.2), custom_call_target="tpu_custom_call" | custom-call | flops 19327352832 | bytes 20971520 | tf_op jit(solution)/shard_map/projection_gradient/pallas_call | solution.py:497
  99.1 3.7 %write_out.1 = (bf16[512,8192]{1,0:T(8,128)(2,1)}, bf16[512,1024]{1,0:T(8,128)(2,1)}, f32[4,1024]{1,0:T(4,128)}) custom-call(bf16[512,8192]{1,0:T(8,128)(2,1)S(1)} %get-tuple-element.9.grad_v, bf16[512,1024]{1,0:T(8,128)(2,1)S(1)} %get-tuple-element.10.new_v, f32[4,1024]{1,0:T(4,128)S(1)} %get-tuple-element.11.right_v), custom_call_target="tpu_custom_call" | custom-call | bytes 9437184 | tf_op jit(solution)/shard_map/write_out/pallas_call | solution.py:532

commit v5 on v4

--- a/solution.py
+++ b/solution.py
@@ -20,7 +20,7 @@
 PIECE = 128
 HALF = 512
 SCALE = float(np.float32(1.0) / np.sqrt(np.float32(TOK * N_FSDP)))
-CUT = 256
+CUT = 192
 ORDER = (
     "w0", "q", "E1", "cot1", "gB0", "P0", "E0b", "xa", "wf", "P1", "ph1", "gB1", "x01", "gB2",
     "m00", "ph2", "E0", "ga", "cot0", "x10", "F11", "x11", "ph3", "F01", "ph4", "cot0b", "gf",
@@ -305,7 +305,7 @@
             need("F00b", "F00c")
         rsend[k] = (product(fid(a, border[k]), 4 + k) + s1r[k].astype(F32)).astype(BF16)
         if k == 0:
-            send("oB", rsend.at[0, low], opp.at[0], at(a, bB))
+            send("oB", rsend.at[0, low], opp.at[0, pl.ds(0, CUT)], at(a, bB))
             send("oA", rsend.at[0, high], opp.at[1, pl.ds(0, CH - CUT)], at(a, bA))
         elif k == 1:
             send("dA", rsend.at[1, high], fin.at[0, high], at(a, bA))
@@ -314,7 +314,7 @@
 
     def task_tA():
         need("oB")
-        rsend[1, low] = (rsend[1, low].astype(F32) + opp[0].astype(F32)).astype(BF16)
+        rsend[1, low] = (rsend[1, low].astype(F32) + opp[0, 0:CUT].astype(F32)).astype(BF16)
         send("tA", rsend.at[1, low], fin.at[0, low], at(a, bA))
 
     def task_tB():
@@ -512,7 +512,7 @@
             pltpu.VMEM((4, CH, D), BF16),
             pltpu.VMEM((4, CH, D), BF16),
             pltpu.VMEM((3, CH, D), BF16),
-            pltpu.VMEM((2, CUT, D), BF16),
+            pltpu.VMEM((2, max(CUT, CH - CUT), D), BF16),
             pltpu.VMEM((2, CH, D), BF16),
             pltpu.VMEM((N_FSDP, CH, D), BF16),
             pltpu.VMEM((CH, D), F32),

time: 103 us -> 102 us (level)
    pallas_call x1, Pallas kernels: 98.5 us -> 97.1 us  [shards(): pl.pallas_call(kernel, out_shape=(pltpu.VMEM((TOK, CH * N_FSDP), BF16), p...]
where the time goes in v5:
time: 102 us
  Pallas kernels  101 us (99%)
    pallas_call x1, Pallas kernels, shards(): pl.pallas_call(kernel, out_shape=(pltpu.VMEM((TOK, CH * N_FSDP), BF16), p...  97.1 us
    pallas_call x1, Pallas kernels, shards(): pl.pallas_call(write_out, out_shape=tuple((jax.ShapeDtypeStruct(r.shape,...  3.67 us

profile of v5, /device:TPU:1, one launch (start us, length us, event | category | flops | bytes accessed | tf_op | source)
XLA Modules:
  0.0 101.6 jit_solution(4377127129642676034)
XLA Ops:
  0.6 97.1 %projection_gradient.1 = (bf16[512,8192]{1,0:T(8,128)(2,1)S(1)}, bf16[512,1024]{1,0:T(8,128)(2,1)S(1)}, f32[4,1024]{1,0:T(4,128)S(1)}) custom-call(f32[4,1024]{1,0:T(4,128)} %seed_ref.1, bf16[512,1024]{1,0:T(8,128)(2,1)} %cot_h.1, bf16[512,8192]{1,0:T(8,128)(2,1)} %ctx_h.1, bf16[512,1024]{1,0:T(8,128)(2,1)} %w_h.1, bf16[512,1024]{1,0:T(8,128)(2,1)} %bitcast.2), custom_call_target="tpu_custom_call" | custom-call | flops 19327352832 | bytes 20971520 | tf_op jit(solution)/shard_map/projection_gradient/pallas_call | solution.py:497
  97.8 3.7 %write_out.1 = (bf16[512,8192]{1,0:T(8,128)(2,1)}, bf16[512,1024]{1,0:T(8,128)(2,1)}, f32[4,1024]{1,0:T(4,128)}) custom-call(bf16[512,8192]{1,0:T(8,128)(2,1)S(1)} %get-tuple-element.9.grad_v, bf16[512,1024]{1,0:T(8,128)(2,1)S(1)} %get-tuple-element.10.new_v, f32[4,1024]{1,0:T(4,128)S(1)} %get-tuple-element.11.right_v), custom_call_target="tpu_custom_call" | custom-call | bytes 9437184 | tf_op jit(solution)/shard_map/write_out/pallas_call | solution.py:532
